TPU v7x, 128 devices: a whole 4x4x4 slice. The times are simulated.
128 devices in a mesh: clip: 32 (over x, z, core), tm: 4 (over y).
Axes of the slice: x: 4, y: 4, z: 4, core: 2. Of those that a mesh axis runs over, the one named last changes fastest.
Arguments:
- tiles: bfloat16 [1024, 16, 8, 8, 128], P('clip', 'tm'), may hold values from -6 to 6
- buckets: int32 [1024, 1], P('clip'), may hold values from 0 to 31; in each aligned block of 32 rows (0 to 31, 32 to 63, ...) at most 2 rows name the same one
- tile_frames: int32 [1024], P('clip'), may hold values from 4 to 16, as said below
- norm_gain: float32 [128], replicated, may hold values from 0.5 to 1.5
- norm_shift: float32 [128], replicated, may hold values from -3 to 3
- conv_weight: bfloat16 [3, 3, 3, 128, 128], replicated, may hold values from -0.109375 to 0.109375
- conv_bias: float32 [128], replicated, may hold values from -2 to 2
Outputs:
- latents: bfloat16 [2048, 16, 8, 8, 128], P('clip', 'tm')
Inputs may be any that keep to these rules, and one draw needn't show every extreme that they name: `buckets`: among the 32 tiles of one reader at most 2 name the same group, and some group gets exactly 2. `tile_frames`: A multiple of 4; the first tile of every reader has all 16 frames.
All inputs are finite; a program needn't handle non-finite values.
Results may differ from a plain program's by a relative error of at most 0.0033.
Values may be sent and summed in bfloat16 or wider, within the bound.
A program may use at most 384 MiB of HBM per device.

v0:
```python
import jax
import jax.numpy as jnp
from jax import lax
from jax.sharding import PartitionSpec as P

GROUPS = 32


def shifted(block, axis, distance):
    devices = range(lax.axis_size(axis))
    route = [(i - distance, i) for i in devices if i - distance in devices]
    return lax.ppermute(block, axis, route)


def encode_local(source, lengths, norm_gain, norm_shift, conv_weight, conv_bias):
    held, frames, height, width, chans = source.shape
    per = chans // GROUPS
    position = lax.axis_index("tm")
    frame_pos = position * frames + jnp.arange(frames, dtype=jnp.int32)
    valid = (frame_pos[None, :] < lengths[:, None]).astype(jnp.float32)
    mask = valid[:, :, None, None, None, None]
    xf = source.astype(jnp.float32).reshape(held, frames, height, width, GROUPS, per)
    count = (jnp.maximum(lengths, 1) * height * width * per).astype(jnp.float32)[:, None]
    total = lax.psum(jnp.sum(xf * mask, axis=(1, 2, 3, 5)), "tm")
    mean = total / count
    centred = (xf - mean[:, None, None, None, :, None]) * mask
    spread = lax.psum(jnp.sum(centred * centred, axis=(1, 2, 3, 5)), "tm")
    var = spread / count
    factor = lax.rsqrt(var + 1e-06)
    count_f = source.shape[1]
    grouped = source.astype(jnp.float32).reshape(held, count_f, height, width, GROUPS, per)
    normed = (grouped - mean[:, None, None, None, :, None]) * factor[:, None, None, None, :, None]
    normed = normed.reshape(held, count_f, height, width, chans) * norm_gain + norm_shift
    act = jax.nn.silu(normed).astype(jnp.bfloat16)
    previous = shifted(act[:, -2:], "tm", 1)
    first = jnp.broadcast_to(act[:, :1], previous.shape)
    previous = jnp.where(position == 0, first, previous)
    series = jnp.concatenate([previous, act], axis=1)
    padded = jnp.pad(series, ((0, 0), (0, 0), (1, 1), (1, 1), (0, 0)))
    result = jnp.zeros((held * frames * height * width, chans), jnp.float32)
    for step in range(3):
        parts = [
            padded[:, step : step + frames, kh : kh + height, kw : kw + width]
            for kh in range(3)
            for kw in range(3)
        ]
        cols = jnp.concatenate(parts, axis=-1).reshape(-1, 9 * chans)
        result = result + jnp.dot(
            cols, conv_weight[step].reshape(9 * chans, chans), preferred_element_type=jnp.float32
        )
    out = (
        source.astype(jnp.float32) + result.reshape(held, frames, height, width, chans) + conv_bias
    )
    return (out * valid[:, :, None, None, None]).astype(jnp.bfloat16)


def on_device(tiles, buckets, tile_frames, norm_gain, norm_shift, conv_weight, conv_bias):
    slots = tiles.shape[0]
    groups_n = lax.axis_size("clip")
    capacity = 2 * slots // groups_n
    bucket = buckets[:, 0]
    onehot = (bucket[:, None] == jnp.arange(groups_n, dtype=jnp.int32)[None, :]).astype(jnp.int32)
    before = jnp.cumsum(onehot, axis=0) - onehot
    rank = jnp.sum(before * onehot, axis=1)
    place = bucket * capacity + rank
    empty = jnp.zeros((groups_n * capacity,) + tiles.shape[1:], jnp.bfloat16)
    outgoing = empty.at[place].set(tiles)
    out_len = jnp.zeros((groups_n * capacity,), jnp.int32).at[place].set(tile_frames)
    arrived, lengths = (
        lax.all_to_all(outgoing, "clip", split_axis=0, concat_axis=0, tiled=True),
        lax.all_to_all(out_len, "clip", split_axis=0, concat_axis=0, tiled=True),
    )
    return encode_local(arrived, lengths, norm_gain, norm_shift, conv_weight, conv_bias)


def solution(mesh):
    in_specs = (P("clip", "tm", None, None, None), P("clip", None), P("clip"), P(), P(), P(), P())
    out_specs = P("clip", "tm", None, None, None)
    return jax.shard_map(
        on_device, mesh=mesh, in_specs=in_specs, out_specs=out_specs, check_vma=False
    )
```

profile of v0, /device:TPU:40, one launch (start us, length us, event | category | flops | bytes accessed | tf_op | source)
XLA Modules:
  0.0 327.4 jit_solution(14218097756801380547)
XLA Ops:
  3.8 8.0 %all-to-all-start.1 = ((s32[32,2,1]{1,2,0:T(1,128)}), s32[32,2,1]{1,2,0:T(1,128)S(1)}, u32[]{:S(2)}, u32[]{:S(2)}) async-start(s32[32,2,1]{1,2,0:T(1,128)} %bitcast.3), calls=%async_computation.1 | async-start | bytes 32768 | tf_op jit(solution)/shard_map/all_to_all | solution.py:71
  14.9 6.2 %scatter_fusion = bf16[64,4,8,8,128]{4,3,2,1,0:T(8,128)(2,1)} fusion(bf16[64,4,8,8,128]{4,3,2,1,0:T(8,128)(2,1)} %broadcast_in_dim.8, s32[32]{0:T(128)S(1)} %fusion.45, bf16[32,4,8,8,128]{4,3,2,1,0:T(8,128)(2,1)} %param.7), kind=kCustom, calls=%fused_computation | custom fusion | bytes 6291584 | tf_op jit(solution)/shard_map/scatter | solution.py:67
  21.1 7.6 %all-to-all-start = ((bf16[64,4,8,8,128]{4,3,2,1,0:T(8,128)(2,1)}), bf16[64,4,8,8,128]{4,3,2,1,0:T(8,128)(2,1)}, u32[]{:S(2)}, u32[]{:S(2)}) async-start(bf16[64,4,8,8,128]{4,3,2,1,0:T(8,128)(2,1)} %scatter_fusion), calls=%async_computation | async-start | bytes 8388608 | tf_op jit(solution)/shard_map/all_to_all | solution.py:70
  30.3 52.9 %all-to-all-done = bf16[64,4,8,8,128]{4,3,2,1,0:T(8,128)(2,1)} async-done(((bf16[64,4,8,8,128]{4,3,2,1,0:T(8,128)(2,1)}), bf16[64,4,8,8,128]{4,3,2,1,0:T(8,128)(2,1)}, u32[]{:S(2)}, u32[]{:S(2)}) %all-to-all-start) | async-done | bytes 4194336 | tf_op jit(solution)/shard_map/all_to_all | solution.py:70
  86.8 14.1 %psum.14 = f32[64,32]{0,1:T(8,128)S(1)} all-reduce(f32[64,32]{0,1:T(8,128)S(1)} %reduce_sum.47), channel_id=1, replica_groups=mesh['clip'=32,'tm'=4] {'tm'}, use_global_device_ids=true, to_apply=%region_6.7 | all-reduce | flops 2048 | bytes 16384 | tf_op jit(solution)/shard_map/psum | solution.py:24
  104.3 16.4 %psum.15 = f32[64,32]{0,1:T(8,128)S(1)} all-reduce(f32[64,32]{0,1:T(8,128)S(1)} %reduce_sum.50), channel_id=1, replica_groups=mesh['clip'=32,'tm'=4] {'tm'}, use_global_device_ids=true, to_apply=%region_9.10 | all-reduce | flops 2048 | bytes 16384 | tf_op jit(solution)/shard_map/psum | solution.py:27
  120.8 4.7 %fusion.11 = bf16[64,4,8,8,128]{4,3,2,1,0:T(8,128)(2,1)S(1)} fusion(bf16[64,4,8,8,128]{4,3,2,1,0:T(8,128)(2,1)} %all-to-all-done, f32[128]{0:T(128)S(1)} %copy-done.2, f32[128]{0:T(128)S(1)} %copy-done.3, f32[64,128]{1,0:T(8,128)S(1)} %copy.20, f32[64,128]{1,0:T(8,128)S(1)} %copy.18), kind=kLoop, calls=%fused_computation.45 | loop fusion | flops 20971520 | bytes 8455168 | tf_op jit(solution)/shard_map/convert_element_type | solution.py:34
  133.1 36.2 %collective-permute-done = bf16[64,2,8,8,128]{4,3,2,1,0:T(8,128)(2,1)} collective-permute-done((bf16[64,2,8,8,128]{4,3,2,1,0:T(8,128)(2,1)S(1)}, bf16[64,2,8,8,128]{4,3,2,1,0:T(8,128)(2,1)}, u32[]{:S(2)}, u32[]{:S(2)}) %collective-permute-start) | collective-permute-done | bytes 2097184 | tf_op jit(solution)/shard_map/ppermute | solution.py:12
  181.6 3.6 %fusion.39 = bf16[64,4,8,8,1152]{4,3,2,1,0:T(8,128)(2,1)} fusion(bf16[64,4,8,8,1152]{4,3,2,1,0:T(8,128)(2,1)} %fusion.38, bf16[64,6,8,8,128]{4,3,2,1,0:T(8,128)(2,1)S(1)} %pad_maximum_fusion), kind=kLoop, calls=%fused_computation.75 | loop fusion | bytes 10485760
  185.1 6.3 %constant_dynamic-update-slice_fusion = bf16[64,4,8,8,1152]{4,3,2,1,0:T(8,128)(2,1)} fusion(bf16[64,4,8,8,1152]{4,3,2,1,0:T(8,128)(2,1)} %fusion.39, f32[128]{0:T(128)S(1)} %copy-done.2, f32[128]{0:T(128)S(1)} %copy-done.3, f32[64,128]{1,0:T(8,128)S(1)} %copy.20, f32[64,128]{1,0:T(8,128)S(1)} %copy.18, bf16[64,4,8,8,128]{4,3,2,1,0:T(8,128)(2,1)} %all-to-all-done), kind=kLoop, calls=%fused_computation.82 | loop fusion | flops 20971520 | bytes 8455168
  191.4 3.5 %fusion.40 = bf16[64,4,8,8,1152]{4,3,2,1,0:T(8,128)(2,1)} fusion(bf16[64,4,8,8,1152]{4,3,2,1,0:T(8,128)(2,1)} %constant_dynamic-update-slice_fusion, bf16[64,6,8,8,128]{4,3,2,1,0:T(8,128)(2,1)S(1)} %pad_maximum_fusion), kind=kLoop, calls=%fused_computation.76 | loop fusion | bytes 10485760
  198.3 4.4 %fusion.42 = (bf16[64,4,8,8,1152]{4,3,2,1,0:T(8,128)(2,1)}, bf16[64,4,8,8,1152]{4,3,2,1,0:T(8,128)(2,1)}) fusion(bf16[64,4,8,8,1152]{4,3,2,1,0:T(8,128)(2,1)} %fusion.41, bf16[64,6,8,8,128]{4,3,2,1,0:T(8,128)(2,1)S(1)} %pad_maximum_fusion), kind=kLoop, calls=%fused_computation.78 | loop fusion | bytes 14680064
  202.7 5.7 %fusion.43 = (bf16[64,4,8,8,1152]{4,3,2,1,0:T(8,128)(2,1)}, bf16[64,4,8,8,1152]{4,3,2,1,0:T(8,128)(2,1)}, bf16[64,4,8,8,1152]{4,3,2,1,0:T(8,128)(2,1)}) fusion(bf16[64,4,8,8,1152]{4,3,2,1,0:T(8,128)(2,1)} %get-tuple-element.8, bf16[64,6,8,8,128]{4,3,2,1,0:T(8,128)(2,1)S(1)} %pad_maximum_fusion, bf16[64,4,8,8,1152]{4,3,2,1,0:T(8,128)(2,1)} %get-tuple-element.9), kind=kLoop, calls=%fused_computation.79 | loop fusion | bytes 18874368 | tf_op jit(solution)/shard_map/concatenate | solution.py:47
  214.9 4.0 %fusion.31 = bf16[64,4,8,8,1152]{4,3,2,1,0:T(8,128)(2,1)} fusion(bf16[64,4,8,8,1152]{4,3,2,1,0:T(8,128)(2,1)} %fusion.30, bf16[64,6,8,8,128]{4,3,2,1,0:T(8,128)(2,1)S(1)} %pad_maximum_fusion), kind=kLoop, calls=%fused_computation.67 | loop fusion | bytes 10485760
  221.5 4.0 %fusion.32 = bf16[64,4,8,8,1152]{4,3,2,1,0:T(8,128)(2,1)} fusion(bf16[64,4,8,8,1152]{4,3,2,1,0:T(8,128)(2,1)} %fusion.19, bf16[64,6,8,8,128]{4,3,2,1,0:T(8,128)(2,1)S(1)} %pad_maximum_fusion), kind=kLoop, calls=%fused_computation.68 | loop fusion | bytes 10485760
  225.4 3.5 %fusion.33 = bf16[64,4,8,8,1152]{4,3,2,1,0:T(8,128)(2,1)} fusion(bf16[64,4,8,8,1152]{4,3,2,1,0:T(8,128)(2,1)} %fusion.32, bf16[64,6,8,8,128]{4,3,2,1,0:T(8,128)(2,1)S(1)} %pad_maximum_fusion), kind=kLoop, calls=%fused_computation.69 | loop fusion | bytes 10485760
  232.1 4.7 %fusion.35 = (bf16[64,4,8,8,1152]{4,3,2,1,0:T(8,128)(2,1)}, bf16[64,4,8,8,1152]{4,3,2,1,0:T(8,128)(2,1)}) fusion(bf16[64,4,8,8,1152]{4,3,2,1,0:T(8,128)(2,1)} %fusion.34, bf16[64,6,8,8,128]{4,3,2,1,0:T(8,128)(2,1)S(1)} %pad_maximum_fusion, bf16[64,4,8,8,1152]{4,3,2,1,0:T(8,128)(2,1)} %get-tuple-element.6), kind=kLoop, calls=%fused_computation.71 | loop fusion | bytes 14680064 | tf_op jit(solution)/shard_map/concatenate | solution.py:47
  236.8 3.6 %fusion.23 = bf16[64,4,8,8,1152]{4,3,2,1,0:T(8,128)(2,1)} fusion(bf16[64,4,8,8,1152]{4,3,2,1,0:T(8,128)(2,1)} %get-tuple-element.11, bf16[64,6,8,8,128]{4,3,2,1,0:T(8,128)(2,1)S(1)} %pad_maximum_fusion), kind=kLoop, calls=%fused_computation.59 | loop fusion | bytes 10485760
  242.7 3.5 %fusion.24 = bf16[64,4,8,8,1152]{4,3,2,1,0:T(8,128)(2,1)} fusion(bf16[64,4,8,8,1152]{4,3,2,1,0:T(8,128)(2,1)} %fusion.17, bf16[64,6,8,8,128]{4,3,2,1,0:T(8,128)(2,1)S(1)} %pad_maximum_fusion), kind=kLoop, calls=%fused_computation.60 | loop fusion | bytes 10485760
  252.6 3.4 %fusion.27 = bf16[64,4,8,8,1152]{4,3,2,1,0:T(8,128)(2,1)} fusion(bf16[64,4,8,8,1152]{4,3,2,1,0:T(8,128)(2,1)} %fusion.26, bf16[64,6,8,8,128]{4,3,2,1,0:T(8,128)(2,1)S(1)} %pad_maximum_fusion), kind=kLoop, calls=%fused_computation.63 | loop fusion | bytes 10485760 | tf_op jit(solution)/shard_map/concatenate | solution.py:47
  256.1 19.0 %fusion.49 = f32[16384,128]{1,0:T(8,128)} fusion(bf16[16384,1152]{1,0:T(8,128)(2,1)} %bitcast.30, bf16[1152,128]{1,0:T(8,128)(2,1)S(1)} %bitcast.34), kind=kOutput, calls=%fused_computation.97 | convolution fusion | flops 4831838208 | bytes 46432256 | tf_op jit(solution)/shard_map/dot_general | solution.py:48
  275.1 22.3 %convolution_add_fusion.1 = f32[16384,128]{1,0:T(8,128)} fusion(f32[16384,128]{1,0:T(8,128)} %fusion.49, bf16[16384,1152]{1,0:T(8,128)(2,1)} %bitcast.28, bf16[1152,128]{1,0:T(8,128)(2,1)S(1)} %bitcast.33), kind=kOutput, calls=%fused_computation.27 | convolution fusion | flops 4833935360 | bytes 54820864 | tf_op jit(solution)/shard_map/dot_general | solution.py:48
  297.4 22.6 %convolution_add_fusion = f32[16384,128]{1,0:T(8,128)} fusion(f32[16384,128]{1,0:T(8,128)} %convolution_add_fusion.1, bf16[16384,1152]{1,0:T(8,128)(2,1)} %bitcast.29, bf16[1152,128]{1,0:T(8,128)(2,1)S(1)} %bitcast.32), kind=kOutput, calls=%fused_computation.26 | convolution fusion | flops 4833935360 | bytes 54820864 | tf_op jit(solution)/shard_map/dot_general | solution.py:48
  320.0 6.9 %fusion.15 = bf16[64,4,8,8,128]{4,3,2,1,0:T(8,128)(2,1)} fusion(f32[64,4,8,8,128]{4,3,2,1,0:T(8,128)} %bitcast.31, bf16[64,4,8,8,128]{4,3,2,1,0:T(8,128)(2,1)} %all-to-all-done, f32[128]{0:T(128)S(1)} %copy-done.4, f32[64,4]{1,0:T(8,128)S(1)} %copy.16), kind=kLoop, calls=%fused_computation.49 | loop fusion | flops 10485760 | bytes 16778752 | tf_op jit(solution)/shard_map/convert_element_type | solution.py:54
  (54 shorter events, 59.4 us)
Async XLA Ops:
  3.8 17.3 %all-to-all-start.1 = ((s32[32,2,1]{1,2,0:T(1,128)}), s32[32,2,1]{1,2,0:T(1,128)S(1)}, u32[]{:S(2)}, u32[]{:S(2)}) async-start(s32[32,2,1]{1,2,0:T(1,128)} %bitcast.3), calls=%async_computation.1 | async-start | bytes 32768 | tf_op jit(solution)/shard_map/all_to_all | solution.py:71
  21.1 99.7 %copy-start.2 = (f32[128]{0:T(128)S(1)}, f32[128]{0:T(128)}, u32[]{:S(2)}) copy-start(f32[128]{0:T(128)} %param.11) | copy-start | bytes 1540
  21.1 99.7 %copy-start.3 = (f32[128]{0:T(128)S(1)}, f32[128]{0:T(128)}, u32[]{:S(2)}) copy-start(f32[128]{0:T(128)} %param.10) | copy-start | bytes 1540
  21.1 62.1 %all-to-all-start = ((bf16[64,4,8,8,128]{4,3,2,1,0:T(8,128)(2,1)}), bf16[64,4,8,8,128]{4,3,2,1,0:T(8,128)(2,1)}, u32[]{:S(2)}, u32[]{:S(2)}) async-start(bf16[64,4,8,8,128]{4,3,2,1,0:T(8,128)(2,1)} %scatter_fusion), calls=%async_computation | async-start | bytes 8388608 | tf_op jit(solution)/shard_map/all_to_all | solution.py:70
  125.5 2.0 copy-start
  127.7 41.7 %collective-permute-start = (bf16[64,2,8,8,128]{4,3,2,1,0:T(8,128)(2,1)S(1)}, bf16[64,2,8,8,128]{4,3,2,1,0:T(8,128)(2,1)}, u32[]{:S(2)}, u32[]{:S(2)}) collective-permute-start(bf16[64,2,8,8,128]{4,3,2,1,0:T(8,128)(2,1)S(1)} %slice.129), channel_id=1, source_target_pairs={{0,1},{1,2},{2,3},{4,5},{5,6},{6,7},{8,9},{9,10},{10,11},{12,13},{... | collective-permute-start | bytes 6291464 | tf_op jit(solution)/shard_map/ppermute | solution.py:12
  130.3 40.8 %copy-start.1 = (bf16[64,4,8,8,128]{4,3,2,1,0:T(8,128)(2,1)S(1)}, bf16[64,4,8,8,128]{4,3,2,1,0:T(8,128)(2,1)}, u32[]{:S(2)}) copy-start(bf16[64,4,8,8,128]{4,3,2,1,0:T(8,128)(2,1)} %copy-done) | copy-start | bytes 12582916
  297.4 22.6 %copy-start.4 = (f32[128]{0:T(128)S(1)}, f32[128]{0:T(128)}, u32[]{:S(2)}) copy-start(f32[128]{0:T(128)} %param.13) | copy-start | bytes 1540
where the time goes:
time: 333 us; the launch traced here: 327 us
  local copies, waits for them, and re-layouts  90.2 us (27%)
  waiting for transfers between devices  89.1 us (27%)
  matrix products  63.9 us (19%)
  other arithmetic  34.7 us (10%)
  blocking collectives  30.5 us (9%)
  starting transfers between devices  18.2 us (5%)
    dot_general x3, matrix products, encode_local(): jnp.dot(cols, conv_weight[step].reshape(9 * chans, chans), preferred_elem...  63.9 us
    unnamed x27, local copies, waits for them, and re-layouts  61.5 us
    all_to_all x1, waiting for transfers between devices, on_device(): lax.all_to_all(outgoing, 'clip', split_axis=0, concat_axis=0, tiled=True)  52.9 us
    ppermute x1, waiting for transfers between devices, shifted(): return lax.ppermute(block, axis, route)  36.2 us
    psum x1, blocking collectives, encode_local(): spread = lax.psum(jnp.sum(centred * centred, axis=(1, 2, 3, 5)), 'tm')  16.4 us
    psum x1, blocking collectives, encode_local(): total = lax.psum(jnp.sum(xf * mask, axis=(1, 2, 3, 5)), 'tm')  14.1 us
    concatenate x3, local copies, waits for them, and re-layouts, encode_local(): cols = jnp.concatenate(parts, axis=-1).reshape(-1, 9 * chans)  13.8 us
    unnamed x3, other arithmetic  11.1 us
  transfers between devices with their start and end apart: 3, of which 2 were waited for; matrix products, arithmetic and copies ran while one was open for 4% of the time, Pallas kernels for 0%

commit v1 on v0

v1 whole, which is shorter than its diff:
```python
import jax
import jax.numpy as jnp
from jax import lax
from jax.experimental import pallas as pl
from jax.experimental.pallas import tpu as pltpu
from jax.sharding import PartitionSpec as P

MESH = pl.DeviceIdType.MESH
CLIP, TM = 32, 4
TILES, CELLS, CHANS = 32, 64, 128
ROWS = 4 * CELLS
PAIRS = TILES // 2


def target(k):
    me = lax.axis_index("clip")
    core, z, x = me % 2, (me // 2) % 4, me // 8
    dc, a = k // 16, k % 16
    dx = a % 4
    dz = (a + a // 4) % 4
    return (((x + dx) % 4) * 4 + (z + dz) % 4) * 2 + (core + dc) % 2


def place_of(group):
    me = lax.axis_index("clip")
    core, z, x = me % 2, (me // 2) % 4, me // 8
    dc = (group % 2 - core + 2) % 2
    dx = (group // 8 - x + 4) % 4
    dz = ((group // 2) % 4 - z + 4) % 4
    k = dc * 16 + dx + 4 * ((dz - dx + 4) % 4)
    return (k + 31) % 32


def group_sum(v):
    lane = lax.broadcasted_iota(jnp.int32, v.shape, 1)
    for step in (1, 2):
        up = pltpu.roll(v, CHANS - step, 1)
        down = pltpu.roll(v, step, 1)
        v = v + jnp.where((lane // step) % 2 == 0, up, down)
    return v


def column_of(row):
    wide = jnp.broadcast_to(row, (TILES, TILES))
    r = lax.broadcasted_iota(jnp.int32, (TILES, TILES), 0)
    c = lax.broadcasted_iota(jnp.int32, (TILES, TILES), 1)
    return jnp.sum(jnp.where(r == c, wide, 0), axis=1, keepdims=True)


def kernel(
    x_hbm, bucket_ref, frames_ref, frames_smem, gain_ref, shift_ref, w_ref, bias_ref, out_ref,
    x_s, halo_out, halo_in, stats, mean_s, scale_s, acts, wide_w, done, send, table_v, table,
    local_sem, halo_ssem, halo_rsem, stat_ssem, stat_rsem, out_ssem, out_rsem,
):
    me, pos = lax.axis_index("clip"), lax.axis_index("tm")
    x_copy = pltpu.make_async_copy(x_hbm, x_s, local_sem.at[0])
    x_copy.start()

    barrier = pltpu.get_barrier_semaphore()

    @pl.loop(1, CLIP)
    def _(k):
        pl.semaphore_signal(barrier, inc=1, device_id={"clip": target(k)}, device_id_type=MESH)

    for d in range(1, TM):
        pl.semaphore_signal(barrier, inc=1, device_id={"tm": (pos + d) % TM}, device_id_type=MESH)

    step_row = place_of(bucket_ref[...])
    step_col = column_of(step_row)
    r = lax.broadcasted_iota(jnp.int32, (TILES, TILES), 0)
    c = lax.broadcasted_iota(jnp.int32, (TILES, TILES), 1)
    other = jnp.broadcast_to(step_row, (TILES, TILES))
    mine = jnp.broadcast_to(step_col, (TILES, TILES))
    ahead = jnp.where((other < mine) | ((other == mine) & (c < r)), 1, 0)
    place_col = jnp.sum(ahead, axis=1, keepdims=True)
    lanes = lax.broadcasted_iota(jnp.int32, (TILES, CHANS), 1)
    tiles_down = lax.broadcasted_iota(jnp.int32, (TILES, CHANS), 0)
    order = jnp.sum(jnp.where(place_col == lanes, tiles_down, 0), axis=0, keepdims=True)
    start = jnp.sum(jnp.where(step_col < lanes, 1, 0), axis=0, keepdims=True)
    table_v[...] = jnp.zeros_like(table_v)
    table_v[0:1, :] = order
    table_v[1:2, :] = start
    table_copy = pltpu.make_async_copy(table_v, table, local_sem.at[1])
    table_copy.start()

    zeros_w = jnp.zeros((CHANS, CHANS), jnp.bfloat16)
    for kt in range(3):
        for kw in range(3):
            base = (kt * 3 + kw) * 4 * CHANS
            for j in range(4):
                rows = pl.ds(base + j * CHANS, CHANS)
                wide_w[rows, 0:CHANS] = w_ref[kt, j, kw] if j < 3 else zeros_w
                wide_w[rows, CHANS : 2 * CHANS] = w_ref[kt, j - 1, kw] if j > 0 else zeros_w
    pad = jnp.zeros((6, 16, CHANS), jnp.bfloat16)
    for kw in range(3):
        acts[kw, 0, :, 0] = pad
        acts[kw, 1, :, 4] = pad

    x_copy.wait()

    @pl.loop(0, TILES)
    def _(t):
        xf = x_s[t].astype(jnp.float32)
        m = jnp.sum(xf, axis=0, keepdims=True) * (1.0 / ROWS)
        dev = xf - m
        stats[pos, 0, pl.ds(t, 1), :] = m
        stats[pos, 1, pl.ds(t, 1), :] = jnp.sum(dev * dev, axis=0, keepdims=True)

    pl.semaphore_wait(barrier, CLIP - 1 + TM - 1)

    def stat_copy(d, there):
        return pltpu.make_async_remote_copy(
            src_ref=stats.at[pos],
            dst_ref=stats.at[there],
            send_sem=stat_ssem.at[d],
            recv_sem=stat_rsem.at[d],
            device_id={"tm": (pos + d) % TM},
            device_id_type=MESH,
        )

    for d in range(1, TM):
        stat_copy(d, pos).start()

    def halo_copy(m):
        return pltpu.make_async_remote_copy(
            src_ref=halo_out.at[m],
            dst_ref=halo_in.at[m],
            send_sem=halo_ssem.at[m],
            recv_sem=halo_rsem.at[m],
            device_id={"tm": (pos + 1) % TM},
            device_id_type=MESH,
        )

    table_copy.wait()

    @pl.loop(0, PAIRS)
    def _(m):
        for i in range(2):
            halo_out[m, i] = x_s[table[0, 2 * m + i], ROWS // 2 : ROWS, :]
        halo_copy(m).start()

    for d in range(1, TM):
        stat_copy(d, (pos + TM - d) % TM).wait_recv()

    length = column_of(frames_ref[...])
    total = jnp.zeros((TILES, CHANS), jnp.float32)
    weights = [jnp.where(length > 4 * j, 1.0, 0.0) for j in range(TM)]
    parts = weights[0] + weights[1] + weights[2] + weights[3]
    for j in range(TM):
        total = total + stats[j, 0] * weights[j]
    mean = group_sum(total) / (parts * 4.0)
    spread = jnp.zeros((TILES, CHANS), jnp.float32)
    for j in range(TM):
        dev = stats[j, 0] - mean
        spread = spread + (stats[j, 1] + float(ROWS) * (dev * dev)) * weights[j]
    var = group_sum(spread) / (parts * (4.0 * ROWS))
    mean_s[...] = mean
    scale_s[...] = lax.rsqrt(var + 1e-06) * (0.5 * gain_ref[...])

    half_shift = 0.5 * shift_ref[...]
    bias = bias_ref[...]

    def fill(i, slot, at, held):
        got = done[jnp.minimum(at, TILES - 1)]
        send[i, slot] = jnp.where(held, got, jnp.zeros_like(got))

    def out_copy(i):
        return pltpu.make_async_remote_copy(
            src_ref=send.at[i],
            dst_ref=out_ref.at[me],
            send_sem=out_ssem.at[i],
            recv_sem=out_rsem.at[i],
            device_id={"clip": target(i + 1)},
            device_id_type=MESH,
        )

    def fill_both(i):
        first, after = table[1, i], table[1, i + 1]
        fill(i, 0, first, after > first)
        fill(i, 1, first + 1, after > first + 1)

    @pl.loop(0, PAIRS)
    def _(m):
        halo_copy(m).wait_recv()
        tiles = [table[0, 2 * m + i] for i in range(2)]
        series = []
        for i, t in enumerate(tiles):
            xb = x_s[t].astype(jnp.float32).reshape(4, 8, 8, CHANS)
            hb = halo_in[m, i].astype(jnp.float32).reshape(2, 8, 8, CHANS)
            hb = jnp.where(pos == 0, jnp.broadcast_to(xb[0:1], hb.shape), hb)
            raw = jnp.concatenate([hb, xb], axis=0)
            mean_t = mean_s[pl.ds(t, 1), :].reshape(1, 1, 1, CHANS)
            scale_t = scale_s[pl.ds(t, 1), :].reshape(1, 1, 1, CHANS)
            h = (raw - mean_t) * scale_t + half_shift.reshape(1, 1, 1, CHANS)
            series.append((h * jnp.tanh(h) + h).reshape(48, 8, CHANS))
        w = lax.broadcasted_iota(jnp.int32, (48, 8, CHANS), 1)
        for kw in range(3):
            moved = []
            for act in series:
                if kw == 0:
                    act = jnp.where(w == 0, 0.0, pltpu.roll(act, 1, 1))
                if kw == 2:
                    act = jnp.where(w == 7, 0.0, pltpu.roll(act, 7, 1))
                moved.append(act.reshape(6, 8, 1, 8, CHANS))
            both = jnp.concatenate(moved, axis=2).reshape(6, 4, 2, 16, CHANS).astype(jnp.bfloat16)
            acts[kw, 1, :, 0:4] = both[:, :, 0]
            acts[kw, 0, :, 1:5] = both[:, :, 1]
        cols = []
        for kt in range(3):
            for kw in range(3):
                for j in range(4):
                    part = acts[kw, j % 2, kt : kt + 4, j // 2 : j // 2 + 4]
                    cols.append(part.reshape(256, CHANS))
        conv = jnp.dot(
            jnp.concatenate(cols, axis=1), wide_w[...], preferred_element_type=jnp.float32
        )
        rows = [conv[:, 0:CHANS].reshape(4, 4, 2, 8, CHANS), conv[:, CHANS:].reshape(4, 4, 2, 8, CHANS)]
        for i, t in enumerate(tiles):
            xb = x_s[t].astype(jnp.float32)
            both = jnp.concatenate([v[:, :, i : i + 1] for v in rows], axis=2).reshape(ROWS, CHANS)
            res = xb + both + bias
            valid = frames_smem[t] > 4 * pos
            done[2 * m + i] = jnp.where(valid, res, jnp.zeros_like(res)).astype(jnp.bfloat16)
        fill_both(m)
        out_copy(m).start()

    @pl.loop(PAIRS, CLIP - 1)
    def _(i):
        fill_both(i)
        out_copy(i).start()

    fill_both(CLIP - 1)
    own = pltpu.make_async_copy(send.at[CLIP - 1], out_ref.at[me], local_sem.at[2])
    own.start()

    for d in range(1, TM):
        stat_copy(d, pos).wait_send()

    @pl.loop(0, PAIRS)
    def _(m):
        halo_copy(m).wait_send()

    @pl.loop(0, CLIP - 1)
    def _(i):
        out_copy(i).wait_send()

    @pl.loop(0, CLIP - 1)
    def _(i):
        out_copy(i).wait_recv()

    own.wait()


def on_device(tiles, buckets, tile_frames, norm_gain, norm_shift, conv_weight, conv_bias):
    vmem = pl.BlockSpec(memory_space=pltpu.VMEM)
    smem = pl.BlockSpec(memory_space=pltpu.SMEM)
    any_ = pl.BlockSpec(memory_space=pl.ANY)
    bf16, f32 = jnp.bfloat16, jnp.float32
    out = pl.pallas_call(
        kernel,
        out_shape=jax.ShapeDtypeStruct((CLIP, 2, ROWS, CHANS), bf16),
        in_specs=[any_, vmem, vmem, smem, vmem, vmem, vmem, vmem],
        out_specs=any_,
        scratch_shapes=[
            pltpu.VMEM((TILES, ROWS, CHANS), bf16),
            pltpu.VMEM((PAIRS, 2, ROWS // 2, CHANS), bf16),
            pltpu.VMEM((PAIRS, 2, ROWS // 2, CHANS), bf16),
            pltpu.VMEM((TM, 2, TILES, CHANS), f32),
            pltpu.VMEM((TILES, CHANS), f32),
            pltpu.VMEM((TILES, CHANS), f32),
            pltpu.VMEM((3, 2, 6, 5, 16, CHANS), bf16),
            pltpu.VMEM((36 * CHANS, 2 * CHANS), bf16),
            pltpu.VMEM((TILES, ROWS, CHANS), bf16),
            pltpu.VMEM((CLIP, 2, ROWS, CHANS), bf16),
            pltpu.VMEM((8, CHANS), jnp.int32),
            pltpu.SMEM((8, CHANS), jnp.int32),
            pltpu.SemaphoreType.DMA((3,)),
            pltpu.SemaphoreType.DMA((PAIRS,)),
            pltpu.SemaphoreType.DMA((PAIRS,)),
            pltpu.SemaphoreType.DMA((TM,)),
            pltpu.SemaphoreType.DMA((TM,)),
            pltpu.SemaphoreType.DMA((CLIP,)),
            pltpu.SemaphoreType.DMA((CLIP,)),
        ],
        compiler_params=pltpu.CompilerParams(
            collective_id=0, has_side_effects=True, vmem_limit_bytes=40 << 20
        ),
        name="encode_and_send",
    )(
        tiles.reshape(TILES, ROWS, CHANS),
        buckets.reshape(1, TILES),
        tile_frames.reshape(1, TILES),
        tile_frames,
        norm_gain.reshape(1, CHANS),
        norm_shift.reshape(1, CHANS),
        conv_weight,
        conv_bias.reshape(1, CHANS),
    )
    return out.reshape((2 * CLIP,) + tiles.shape[1:])


def solution(mesh):
    in_specs = (P("clip", "tm", None, None, None), P("clip", None), P("clip"), P(), P(), P(), P())
    out_specs = P("clip", "tm", None, None, None)
    return jax.shard_map(
        on_device, mesh=mesh, in_specs=in_specs, out_specs=out_specs, check_vma=False
    )
```

time: 333 us -> 78.8 us (0.24)
  the two profiles are of different devices: /device:TPU:40 before, /device:TPU:33 now
where the time goes in v1:
time: 78.8 us; the launch traced here: 78.6 us
  Pallas kernels  70.5 us (89%)
  local copies, waits for them, and re-layouts  8.05 us (10%)
    pallas_call x1, Pallas kernels, on_device(): pl.pallas_call(kernel, out_shape=jax.ShapeDtypeStruct((CLIP, 2, ROWS, CHA...  70.5 us
    unnamed x15, local copies, waits for them, and re-layouts  8.05 us

profile of v1, /device:TPU:33, one launch (start us, length us, event | category | flops | bytes accessed | tf_op | source)
XLA Modules:
  0.0 78.6 jit_solution(16539217381977198663)
XLA Ops:
  0.0 0.0 copy-start
  0.0 1.6 %copy-done = bf16[32,4,8,8,128]{4,3,2,1,0:T(8,128)(2,1)S(1)} copy-done((bf16[32,4,8,8,128]{4,3,2,1,0:T(8,128)(2,1)S(1)}, bf16[32,4,8,8,128]{4,3,2,1,0:T(8,128)(2,1)}, u32[]{:S(2)}) %copy-start) | copy-done | bytes 2097176
  1.6 0.0 copy-start.1
  1.6 1.2 %copy-done.1 = bf16[3,3,3,128,128]{4,3,2,1,0:T(8,128)(2,1)S(1)} copy-done((bf16[3,3,3,128,128]{4,3,2,1,0:T(8,128)(2,1)S(1)}, bf16[3,3,3,128,128]{4,3,2,1,0:T(8,128)(2,1)}, u32[]{:S(2)}) %copy-start.1) | copy-done | bytes 884760
  2.8 0.0 copy-start.2
  2.8 0.7 copy-done.2
  3.4 0.0 copy-start.3
  3.4 0.7 copy-done.3
  4.1 0.0 copy-start.4
  4.1 0.7 copy-done.4
  4.7 0.0 copy-start.5
  4.7 0.7 copy-done.5
  5.4 0.0 copy-start.6
  5.4 0.7 copy-done.6
  6.0 70.5 %encode_and_send.1 = bf16[32,2,256,128]{3,2,1,0:T(8,128)(2,1)S(1)} custom-call(bf16[32,256,128]{2,1,0:T(8,128)(2,1)S(1)} %bitcast.8, s32[1,32]{1,0:T(1,128)S(1)} %bitcast.10, s32[1,32]{1,0:T(1,128)S(1)} %bitcast.9, s32[32]{0:T(128)S(1)} %copy-done.2, f32[1,128]{1,0:T(1,128)S(1)} %bitcast.11, f32[1,128]{1,0:T(1,128)S(1)} %bitcast.12, ...), custom_call_target="tpu_custom_call" | custom-call | tf_op jit(solution)/shard_map/encode_and_send/pallas_call | solution.py:259
  76.6 2.0 %copy.9 = bf16[64,4,8,8,128]{4,3,2,1,0:T(8,128)(2,1)} copy(bf16[64,4,8,8,128]{4,3,2,1,0:T(8,128)(2,1)S(1)} %bitcast.7) | data formatting | bytes 8388608
Async XLA Ops:
  0.0 1.6 %copy-start = (bf16[32,4,8,8,128]{4,3,2,1,0:T(8,128)(2,1)S(1)}, bf16[32,4,8,8,128]{4,3,2,1,0:T(8,128)(2,1)}, u32[]{:S(2)}) copy-start(bf16[32,4,8,8,128]{4,3,2,1,0:T(8,128)(2,1)} %param.7) | copy-start | bytes 6291460
  1.6 1.2 %copy-start.1 = (bf16[3,3,3,128,128]{4,3,2,1,0:T(8,128)(2,1)S(1)}, bf16[3,3,3,128,128]{4,3,2,1,0:T(8,128)(2,1)}, u32[]{:S(2)}) copy-start(bf16[3,3,3,128,128]{4,3,2,1,0:T(8,128)(2,1)} %w_ref.1) | copy-start | bytes 2654212
  2.8 0.7 copy-start.2
  3.4 0.7 copy-start.3
  4.1 0.7 copy-start.4
  4.7 0.7 copy-start.5
  5.4 0.7 copy-start.6

commit v2 on v1

--- a/solution.py
+++ b/solution.py
@@ -10,20 +10,24 @@
 TILES, CELLS, CHANS = 32, 64, 128
 ROWS = 4 * CELLS
 PAIRS = TILES // 2
+CHUNKS = 4
+
+
+def here():
+    me = lax.axis_index("clip")
+    return lax.div(me, 8), lax.rem(lax.div(me, 2), 4), lax.rem(me, 2)
 
 
 def target(k):
-    me = lax.axis_index("clip")
-    core, z, x = me % 2, (me // 2) % 4, me // 8
-    dc, a = k // 16, k % 16
-    dx = a % 4
-    dz = (a + a // 4) % 4
-    return (((x + dx) % 4) * 4 + (z + dz) % 4) * 2 + (core + dc) % 2
+    x, z, core = here()
+    dc, a = lax.div(k, 16), lax.rem(k, 16)
+    dx = lax.rem(a, 4)
+    dz = a + lax.div(a, 4)
+    return (lax.rem(x + dx, 4) * 4 + lax.rem(z + dz, 4)) * 2 + lax.rem(core + dc, 2)
 
 
 def place_of(group):
-    me = lax.axis_index("clip")
-    core, z, x = me % 2, (me // 2) % 4, me // 8
+    x, z, core = here()
     dc = (group % 2 - core + 2) % 2
     dx = (group // 8 - x + 4) % 4
     dz = ((group // 2) % 4 - z + 4) % 4
@@ -48,24 +52,52 @@
 
 
 def kernel(
-    x_hbm, bucket_ref, frames_ref, frames_smem, gain_ref, shift_ref, w_ref, bias_ref, out_ref,
-    x_s, halo_out, halo_in, stats, mean_s, scale_s, acts, wide_w, done, send, table_v, table,
-    local_sem, halo_ssem, halo_rsem, stat_ssem, stat_rsem, out_ssem, out_rsem,
+    x_hbm, bucket_hbm, frames_row_hbm, frames_hbm, gain_hbm, shift_hbm, w_hbm, bias_hbm, out_ref,
+    x_s, bucket_s, frames_row, frames_smem, gain_ref, shift_ref, bias_ref,
+    halo_out, halo_in, stats, mean_s, scale_s, acts, wide_w, done, send, table_v, table,
+    x_sem, small_sem, w_sem, local_sem, halo_ssem, halo_rsem, stat_ssem, stat_rsem, out_ssem, out_rsem,
 ):
     me, pos = lax.axis_index("clip"), lax.axis_index("tm")
-    x_copy = pltpu.make_async_copy(x_hbm, x_s, local_sem.at[0])
-    x_copy.start()
+
+    smalls = [
+        (bucket_hbm, bucket_s), (frames_row_hbm, frames_row), (frames_hbm, frames_smem),
+        (gain_hbm, gain_ref), (shift_hbm, shift_ref), (bias_hbm, bias_ref),
+    ]
+    small_copies = [
+        pltpu.make_async_copy(src, dst, small_sem.at[i]) for i, (src, dst) in enumerate(smalls)
+    ]
+    small_copies[0].start()
+    x_copies = []
+    for q in range(CHUNKS):
+        part = pl.ds(q * (TILES // CHUNKS), TILES // CHUNKS)
+        x_copies.append(pltpu.make_async_copy(x_hbm.at[part], x_s.at[part], x_sem.at[q]))
+        x_copies[q].start()
 
     barrier = pltpu.get_barrier_semaphore()
-
-    @pl.loop(1, CLIP)
-    def _(k):
-        pl.semaphore_signal(barrier, inc=1, device_id={"clip": target(k)}, device_id_type=MESH)
-
+    for k in range(1, CLIP):
+        pl.semaphore_signal(
+            barrier, inc=1, device_id={"clip": target(jnp.int32(k))}, device_id_type=MESH
+        )
     for d in range(1, TM):
-        pl.semaphore_signal(barrier, inc=1, device_id={"tm": (pos + d) % TM}, device_id_type=MESH)
-
-    step_row = place_of(bucket_ref[...])
+        there = lax.rem(pos + d, TM)
+        pl.semaphore_signal(barrier, inc=1, device_id={"tm": there}, device_id_type=MESH)
+
+    for copy in small_copies[1:]:
+        copy.start()
+    w_copies = []
+    for kt in range(3):
+        for kw in range(3):
+            for odd in range(2):
+                copy = pltpu.make_async_copy(
+                    w_hbm.at[kt, :, kw],
+                    wide_w.at[kt * 3 + kw, pl.ds(odd, 3), :, pl.ds(odd * CHANS, CHANS)],
+                    w_sem.at[(kt * 3 + kw) * 2 + odd],
+                )
+                copy.start()
+                w_copies.append(copy)
+
+    small_copies[0].wait()
+    step_row = place_of(bucket_s[...])
     step_col = column_of(step_row)
     r = lax.broadcasted_iota(jnp.int32, (TILES, TILES), 0)
     c = lax.broadcasted_iota(jnp.int32, (TILES, TILES), 1)
@@ -83,28 +115,26 @@
     table_copy = pltpu.make_async_copy(table_v, table, local_sem.at[1])
     table_copy.start()
 
-    zeros_w = jnp.zeros((CHANS, CHANS), jnp.bfloat16)
-    for kt in range(3):
-        for kw in range(3):
-            base = (kt * 3 + kw) * 4 * CHANS
-            for j in range(4):
-                rows = pl.ds(base + j * CHANS, CHANS)
-                wide_w[rows, 0:CHANS] = w_ref[kt, j, kw] if j < 3 else zeros_w
-                wide_w[rows, CHANS : 2 * CHANS] = w_ref[kt, j - 1, kw] if j > 0 else zeros_w
+    zeros_w = jnp.zeros((9, CHANS, CHANS), jnp.bfloat16)
+    wide_w[:, 3, :, 0:CHANS] = zeros_w
+    wide_w[:, 0, :, CHANS : 2 * CHANS] = zeros_w
     pad = jnp.zeros((6, 16, CHANS), jnp.bfloat16)
     for kw in range(3):
         acts[kw, 0, :, 0] = pad
         acts[kw, 1, :, 4] = pad
 
-    x_copy.wait()
-
-    @pl.loop(0, TILES)
-    def _(t):
-        xf = x_s[t].astype(jnp.float32)
-        m = jnp.sum(xf, axis=0, keepdims=True) * (1.0 / ROWS)
-        dev = xf - m
-        stats[pos, 0, pl.ds(t, 1), :] = m
-        stats[pos, 1, pl.ds(t, 1), :] = jnp.sum(dev * dev, axis=0, keepdims=True)
+    for q in range(CHUNKS):
+        x_copies[q].wait()
+
+        @pl.loop(q * (TILES // CHUNKS), (q + 1) * (TILES // CHUNKS), unroll=4)
+        def _(t):
+            xf = x_s[t].astype(jnp.float32)
+            pivot = xf[0:1]
+            dev = (xf - pivot).reshape(ROWS // 8, 8, CHANS)
+            first = jnp.sum(jnp.sum(dev, axis=0), axis=0, keepdims=True) * (1.0 / ROWS)
+            second = jnp.sum(jnp.sum(dev * dev, axis=0), axis=0, keepdims=True)
+            stats[pos, 0, pl.ds(t, 1), :] = pivot + first
+            stats[pos, 1, pl.ds(t, 1), :] = jnp.maximum(second - float(ROWS) * (first * first), 0.0)
 
     pl.semaphore_wait(barrier, CLIP - 1 + TM - 1)
 
@@ -114,7 +144,7 @@
             dst_ref=stats.at[there],
             send_sem=stat_ssem.at[d],
             recv_sem=stat_rsem.at[d],
-            device_id={"tm": (pos + d) % TM},
+            device_id={"tm": lax.rem(pos + d, TM)},
             device_id_type=MESH,
         )
 
@@ -127,7 +157,7 @@
             dst_ref=halo_in.at[m],
             send_sem=halo_ssem.at[m],
             recv_sem=halo_rsem.at[m],
-            device_id={"tm": (pos + 1) % TM},
+            device_id={"tm": lax.rem(pos + 1, TM)},
             device_id_type=MESH,
         )
 
@@ -139,10 +169,12 @@
             halo_out[m, i] = x_s[table[0, 2 * m + i], ROWS // 2 : ROWS, :]
         halo_copy(m).start()
 
+    for copy in small_copies[1:]:
+        copy.wait()
     for d in range(1, TM):
-        stat_copy(d, (pos + TM - d) % TM).wait_recv()
-
-    length = column_of(frames_ref[...])
+        stat_copy(d, lax.rem(pos + TM - d, TM)).wait_recv()
+
+    length = column_of(frames_row[...])
     total = jnp.zeros((TILES, CHANS), jnp.float32)
     weights = [jnp.where(length > 4 * j, 1.0, 0.0) for j in range(TM)]
     parts = weights[0] + weights[1] + weights[2] + weights[3]
@@ -159,6 +191,8 @@
 
     half_shift = 0.5 * shift_ref[...]
     bias = bias_ref[...]
+    for copy in w_copies:
+        copy.wait()
 
     def fill(i, slot, at, held):
         got = done[jnp.minimum(at, TILES - 1)]
@@ -212,7 +246,9 @@
                     part = acts[kw, j % 2, kt : kt + 4, j // 2 : j // 2 + 4]
                     cols.append(part.reshape(256, CHANS))
         conv = jnp.dot(
-            jnp.concatenate(cols, axis=1), wide_w[...], preferred_element_type=jnp.float32
+            jnp.concatenate(cols, axis=1),
+            wide_w[...].reshape(36 * CHANS, 2 * CHANS),
+            preferred_element_type=jnp.float32,
         )
         rows = [conv[:, 0:CHANS].reshape(4, 4, 2, 8, CHANS), conv[:, CHANS:].reshape(4, 4, 2, 8, CHANS)]
         for i, t in enumerate(tiles):
@@ -252,28 +288,36 @@
 
 
 def on_device(tiles, buckets, tile_frames, norm_gain, norm_shift, conv_weight, conv_bias):
-    vmem = pl.BlockSpec(memory_space=pltpu.VMEM)
-    smem = pl.BlockSpec(memory_space=pltpu.SMEM)
+    hbm = pl.BlockSpec(memory_space=pltpu.HBM)
     any_ = pl.BlockSpec(memory_space=pl.ANY)
     bf16, f32 = jnp.bfloat16, jnp.float32
     out = pl.pallas_call(
         kernel,
         out_shape=jax.ShapeDtypeStruct((CLIP, 2, ROWS, CHANS), bf16),
-        in_specs=[any_, vmem, vmem, smem, vmem, vmem, vmem, vmem],
+        in_specs=[hbm] * 8,
         out_specs=any_,
         scratch_shapes=[
             pltpu.VMEM((TILES, ROWS, CHANS), bf16),
+            pltpu.VMEM((1, TILES), jnp.int32),
+            pltpu.VMEM((1, TILES), jnp.int32),
+            pltpu.SMEM((TILES,), jnp.int32),
+            pltpu.VMEM((1, CHANS), f32),
+            pltpu.VMEM((1, CHANS), f32),
+            pltpu.VMEM((1, CHANS), f32),
             pltpu.VMEM((PAIRS, 2, ROWS // 2, CHANS), bf16),
             pltpu.VMEM((PAIRS, 2, ROWS // 2, CHANS), bf16),
             pltpu.VMEM((TM, 2, TILES, CHANS), f32),
             pltpu.VMEM((TILES, CHANS), f32),
             pltpu.VMEM((TILES, CHANS), f32),
             pltpu.VMEM((3, 2, 6, 5, 16, CHANS), bf16),
-            pltpu.VMEM((36 * CHANS, 2 * CHANS), bf16),
+            pltpu.VMEM((9, 4, CHANS, 2 * CHANS), bf16),
             pltpu.VMEM((TILES, ROWS, CHANS), bf16),
             pltpu.VMEM((CLIP, 2, ROWS, CHANS), bf16),
             pltpu.VMEM((8, CHANS), jnp.int32),
             pltpu.SMEM((8, CHANS), jnp.int32),
+            pltpu.SemaphoreType.DMA((CHUNKS,)),
+            pltpu.SemaphoreType.DMA((6,)),
+            pltpu.SemaphoreType.DMA((18,)),
             pltpu.SemaphoreType.DMA((3,)),
             pltpu.SemaphoreType.DMA((PAIRS,)),
             pltpu.SemaphoreType.DMA((PAIRS,)),
@@ -287,14 +331,19 @@
         ),
         name="encode_and_send",
     )(
-        tiles.reshape(TILES, ROWS, CHANS),
-        buckets.reshape(1, TILES),
-        tile_frames.reshape(1, TILES),
-        tile_frames,
-        norm_gain.reshape(1, CHANS),
-        norm_shift.reshape(1, CHANS),
-        conv_weight,
-        conv_bias.reshape(1, CHANS),
+        *[
+            pltpu.with_memory_space_constraint(v, pltpu.HBM)
+            for v in (
+                tiles.reshape(TILES, ROWS, CHANS),
+                buckets.reshape(1, TILES),
+                tile_frames.reshape(1, TILES),
+                tile_frames,
+                norm_gain.reshape(1, CHANS),
+                norm_shift.reshape(1, CHANS),
+                conv_weight,
+                conv_bias.reshape(1, CHANS),
+            )
+        ]
     )
     return out.reshape((2 * CLIP,) + tiles.shape[1:])
 

time: 78.8 us -> 71.9 us (0.912)
  the two profiles are of different devices: /device:TPU:33 before, /device:TPU:1 now
where the time goes in v2:
time: 71.9 us; the launch traced here: 71.8 us
  Pallas kernels  69.8 us (97%)
  local copies, waits for them, and re-layouts  2.02 us (3%)
    pallas_call x1, Pallas kernels, on_device(): pl.pallas_call(kernel, out_shape=jax.ShapeDtypeStruct((CLIP, 2, ROWS, CHA...  69.8 us
    unnamed x1, local copies, waits for them, and re-layouts  2.02 us

profile of v2, /device:TPU:1, one launch (start us, length us, event | category | flops | bytes accessed | tf_op | source)
XLA Modules:
  0.0 71.8 jit_solution(17985138245695186486)
XLA Ops:
  0.0 69.8 %encode_and_send.1 = bf16[32,2,256,128]{3,2,1,0:T(8,128)(2,1)S(1)} custom-call(bf16[32,256,128]{2,1,0:T(8,128)(2,1)} %bitcast.8, s32[1,32]{1,0:T(1,128)} %bitcast.10, s32[1,32]{1,0:T(1,128)} %bitcast.9, s32[32]{0:T(128)} %frames_hbm.1, f32[1,128]{1,0:T(1,128)} %bitcast.11, f32[1,128]{1,0:T(1,128)} %bitcast.12, bf16[3,3,3,128,128]{4,3,2,1,0:T(8,128)(2,1)} %w_hbm.1, ...), custom_call_target="tpu_custom_call" | custom-call | tf_op jit(solution)/shard_map/encode_and_send/pallas_call | solution.py:294
  69.8 2.0 %copy.9 = bf16[64,4,8,8,128]{4,3,2,1,0:T(8,128)(2,1)} copy(bf16[64,4,8,8,128]{4,3,2,1,0:T(8,128)(2,1)S(1)} %bitcast.7) | data formatting | bytes 8388608

commit v3 on v2

--- a/solution.py
+++ b/solution.py
@@ -11,6 +11,8 @@
 ROWS = 4 * CELLS
 PAIRS = TILES // 2
 CHUNKS = 4
+EARLY = 4
+SENDS = CLIP - 1 - EARLY
 
 
 def here():
@@ -26,13 +28,21 @@
     return (lax.rem(x + dx, 4) * 4 + lax.rem(z + dz, 4)) * 2 + lax.rem(core + dc, 2)
 
 
+def origin(k):
+    x, z, core = here()
+    dc, a = lax.div(k, 16), lax.rem(k, 16)
+    dx = lax.rem(a, 4)
+    dz = lax.rem(a + lax.div(a, 4), 4)
+    return (lax.rem(x + 4 - dx, 4) * 4 + lax.rem(z + 4 - dz, 4)) * 2 + lax.rem(core + 2 - dc, 2)
+
+
 def place_of(group):
     x, z, core = here()
     dc = (group % 2 - core + 2) % 2
     dx = (group // 8 - x + 4) % 4
     dz = ((group // 2) % 4 - z + 4) % 4
     k = dc * 16 + dx + 4 * ((dz - dx + 4) % 4)
-    return (k + 31) % 32
+    return (k + 31 - EARLY) % 32
 
 
 def group_sum(v):
@@ -55,7 +65,9 @@
     x_hbm, bucket_hbm, frames_row_hbm, frames_hbm, gain_hbm, shift_hbm, w_hbm, bias_hbm, out_ref,
     x_s, bucket_s, frames_row, frames_smem, gain_ref, shift_ref, bias_ref,
     halo_out, halo_in, stats, mean_s, scale_s, acts, wide_w, done, send, table_v, table,
+    raw_out, raw_in, late_halo, late_done, notes_out, notes_in,
     x_sem, small_sem, w_sem, local_sem, halo_ssem, halo_rsem, stat_ssem, stat_rsem, out_ssem, out_rsem,
+    raw_ssem, raw_rsem, late_ssem, late_rsem, notes_ssem, notes_rsem, late_sem,
 ):
     me, pos = lax.axis_index("clip"), lax.axis_index("tm")
 
@@ -123,9 +135,47 @@
         acts[kw, 0, :, 0] = pad
         acts[kw, 1, :, 4] = pad
 
+    def raw_copy(j):
+        return pltpu.make_async_remote_copy(
+            src_ref=raw_out.at[j],
+            dst_ref=raw_in.at[j],
+            send_sem=raw_ssem.at[j],
+            recv_sem=raw_rsem.at[j],
+            device_id={"clip": target(j + 1)},
+            device_id_type=MESH,
+        )
+
+    def early_slots(j):
+        first, after = table[1, CLIP - EARLY + j], table[1, CLIP - EARLY + 1 + j]
+        places = [first, first + 1]
+        return [(table[0, jnp.minimum(at, TILES - 1)], after > at) for at in places]
+
+    table_copy.wait()
+    for copy in x_copies:
+        copy.wait()
+
+    @pl.loop(0, EARLY)
+    def _(j):
+        for i, (t, _) in enumerate(early_slots(j)):
+            raw_out[j, i] = x_s[t]
+
+    pl.semaphore_wait(barrier, CLIP - 1 + TM - 1)
+
+    @pl.loop(0, EARLY)
+    def _(j):
+        raw_copy(j).start()
+
+    def stat_copy(d, there):
+        return pltpu.make_async_remote_copy(
+            src_ref=stats.at[pos],
+            dst_ref=stats.at[there],
+            send_sem=stat_ssem.at[d],
+            recv_sem=stat_rsem.at[d],
+            device_id={"tm": lax.rem(pos + d, TM)},
+            device_id_type=MESH,
+        )
+
     for q in range(CHUNKS):
-        x_copies[q].wait()
-
         @pl.loop(q * (TILES // CHUNKS), (q + 1) * (TILES // CHUNKS), unroll=4)
         def _(t):
             xf = x_s[t].astype(jnp.float32)
@@ -136,18 +186,6 @@
             stats[pos, 0, pl.ds(t, 1), :] = pivot + first
             stats[pos, 1, pl.ds(t, 1), :] = jnp.maximum(second - float(ROWS) * (first * first), 0.0)
 
-    pl.semaphore_wait(barrier, CLIP - 1 + TM - 1)
-
-    def stat_copy(d, there):
-        return pltpu.make_async_remote_copy(
-            src_ref=stats.at[pos],
-            dst_ref=stats.at[there],
-            send_sem=stat_ssem.at[d],
-            recv_sem=stat_rsem.at[d],
-            device_id={"tm": lax.rem(pos + d, TM)},
-            device_id_type=MESH,
-        )
-
     for d in range(1, TM):
         stat_copy(d, pos).start()
 
@@ -160,8 +198,6 @@
             device_id={"tm": lax.rem(pos + 1, TM)},
             device_id_type=MESH,
         )
-
-    table_copy.wait()
 
     @pl.loop(0, PAIRS)
     def _(m):
@@ -204,7 +240,7 @@
             dst_ref=out_ref.at[me],
             send_sem=out_ssem.at[i],
             recv_sem=out_rsem.at[i],
-            device_id={"clip": target(i + 1)},
+            device_id={"clip": target(i + 1 + EARLY)},
             device_id_type=MESH,
         )
 
@@ -213,18 +249,15 @@
         fill(i, 0, first, after > first)
         fill(i, 1, first + 1, after > first + 1)
 
-    @pl.loop(0, PAIRS)
-    def _(m):
-        halo_copy(m).wait_recv()
-        tiles = [table[0, 2 * m + i] for i in range(2)]
+    def unit(tiles):
         series = []
-        for i, t in enumerate(tiles):
-            xb = x_s[t].astype(jnp.float32).reshape(4, 8, 8, CHANS)
-            hb = halo_in[m, i].astype(jnp.float32).reshape(2, 8, 8, CHANS)
+        for cells, before, mean_t, scale_t in tiles:
+            xb = cells.astype(jnp.float32).reshape(4, 8, 8, CHANS)
+            hb = before.astype(jnp.float32).reshape(2, 8, 8, CHANS)
             hb = jnp.where(pos == 0, jnp.broadcast_to(xb[0:1], hb.shape), hb)
             raw = jnp.concatenate([hb, xb], axis=0)
-            mean_t = mean_s[pl.ds(t, 1), :].reshape(1, 1, 1, CHANS)
-            scale_t = scale_s[pl.ds(t, 1), :].reshape(1, 1, 1, CHANS)
+            mean_t = mean_t.reshape(1, 1, 1, CHANS)
+            scale_t = scale_t.reshape(1, 1, 1, CHANS)
             h = (raw - mean_t) * scale_t + half_shift.reshape(1, 1, 1, CHANS)
             series.append((h * jnp.tanh(h) + h).reshape(48, 8, CHANS))
         w = lax.broadcasted_iota(jnp.int32, (48, 8, CHANS), 1)
@@ -250,24 +283,95 @@
             wide_w[...].reshape(36 * CHANS, 2 * CHANS),
             preferred_element_type=jnp.float32,
         )
-        rows = [conv[:, 0:CHANS].reshape(4, 4, 2, 8, CHANS), conv[:, CHANS:].reshape(4, 4, 2, 8, CHANS)]
+        rows = [
+            conv[:, 0:CHANS].reshape(4, 4, 2, 8, CHANS),
+            conv[:, CHANS:].reshape(4, 4, 2, 8, CHANS),
+        ]
+        results = []
+        for i, (cells, _, _, _) in enumerate(tiles):
+            both = jnp.concatenate([v[:, :, i : i + 1] for v in rows], axis=2)
+            results.append(cells.astype(jnp.float32) + both.reshape(ROWS, CHANS) + bias)
+        return results
+
+    def late_copy(j):
+        return pltpu.make_async_remote_copy(
+            src_ref=raw_in.at[j, :, pl.ds(ROWS // 2, ROWS // 2)],
+            dst_ref=late_halo.at[j],
+            send_sem=late_ssem.at[j],
+            recv_sem=late_rsem.at[j],
+            device_id={"tm": lax.rem(pos + 1, TM)},
+            device_id_type=MESH,
+        )
+
+    def notes_copy(j):
+        return pltpu.make_async_remote_copy(
+            src_ref=notes_out.at[j],
+            dst_ref=notes_in.at[j],
+            send_sem=notes_ssem.at[j],
+            recv_sem=notes_rsem.at[j],
+            device_id={"clip": target(j + 1)},
+            device_id_type=MESH,
+        )
+
+    @pl.loop(0, EARLY)
+    def _(j):
+        notes_out[j] = jnp.zeros((8, CHANS), jnp.float32)
+        for i, (t, held) in enumerate(early_slots(j)):
+            notes_out[j, i : i + 1] = mean_s[pl.ds(t, 1), :]
+            notes_out[j, 2 + i : 3 + i] = scale_s[pl.ds(t, 1), :]
+            valid = held & (frames_smem[t] > 4 * pos)
+            notes_out[j, 4 + i : 5 + i] = jnp.where(valid, jnp.ones((1, CHANS)), jnp.zeros((1, CHANS)))
+        notes_copy(j).start()
+
+    @pl.loop(0, PAIRS)
+    def _(m):
+        halo_copy(m).wait_recv()
+        tiles = [table[0, 2 * m + i] for i in range(2)]
+        results = unit(
+            [
+                (x_s[t], halo_in[m, i], mean_s[pl.ds(t, 1), :], scale_s[pl.ds(t, 1), :])
+                for i, t in enumerate(tiles)
+            ]
+        )
         for i, t in enumerate(tiles):
-            xb = x_s[t].astype(jnp.float32)
-            both = jnp.concatenate([v[:, :, i : i + 1] for v in rows], axis=2).reshape(ROWS, CHANS)
-            res = xb + both + bias
             valid = frames_smem[t] > 4 * pos
+            res = results[i]
             done[2 * m + i] = jnp.where(valid, res, jnp.zeros_like(res)).astype(jnp.bfloat16)
         fill_both(m)
         out_copy(m).start()
 
-    @pl.loop(PAIRS, CLIP - 1)
+        @pl.when(m >= PAIRS - EARLY)
+        def _():
+            raw_copy(m - (PAIRS - EARLY)).wait_recv()
+            late_copy(m - (PAIRS - EARLY)).start()
+
+    @pl.loop(PAIRS, SENDS)
     def _(i):
         fill_both(i)
         out_copy(i).start()
 
-    fill_both(CLIP - 1)
-    own = pltpu.make_async_copy(send.at[CLIP - 1], out_ref.at[me], local_sem.at[2])
+    fill_both(SENDS)
+    own = pltpu.make_async_copy(send.at[SENDS], out_ref.at[me], local_sem.at[2])
     own.start()
+
+    def late_out(j):
+        return pltpu.make_async_copy(late_done.at[j], out_ref.at[origin(j + 1)], late_sem.at[j])
+
+    @pl.loop(0, EARLY)
+    def _(j):
+        late_copy(j).wait_recv()
+        notes_copy(j).wait_recv()
+        results = unit(
+            [
+                (raw_in[j, i], late_halo[j, i], notes_in[j, i : i + 1], notes_in[j, 2 + i : 3 + i])
+                for i in range(2)
+            ]
+        )
+        for i in range(2):
+            valid = notes_in[j, 4 + i : 5 + i] > 0.5
+            res = results[i]
+            late_done[j, i] = jnp.where(valid, res, jnp.zeros_like(res)).astype(jnp.bfloat16)
+        late_out(j).start()
 
     for d in range(1, TM):
         stat_copy(d, pos).wait_send()
@@ -276,15 +380,22 @@
     def _(m):
         halo_copy(m).wait_send()
 
-    @pl.loop(0, CLIP - 1)
+    @pl.loop(0, EARLY)
+    def _(j):
+        raw_copy(j).wait_send()
+        late_copy(j).wait_send()
+        notes_copy(j).wait_send()
+        late_out(j).wait()
+
+    own.wait()
+
+    @pl.loop(0, SENDS)
     def _(i):
         out_copy(i).wait_send()
 
-    @pl.loop(0, CLIP - 1)
+    @pl.loop(0, SENDS)
     def _(i):
         out_copy(i).wait_recv()
-
-    own.wait()
 
 
 def on_device(tiles, buckets, tile_frames, norm_gain, norm_shift, conv_weight, conv_bias):
@@ -312,9 +423,15 @@
             pltpu.VMEM((3, 2, 6, 5, 16, CHANS), bf16),
             pltpu.VMEM((9, 4, CHANS, 2 * CHANS), bf16),
             pltpu.VMEM((TILES, ROWS, CHANS), bf16),
-            pltpu.VMEM((CLIP, 2, ROWS, CHANS), bf16),
+            pltpu.VMEM((SENDS + 1, 2, ROWS, CHANS), bf16),
             pltpu.VMEM((8, CHANS), jnp.int32),
             pltpu.SMEM((8, CHANS), jnp.int32),
+            pltpu.VMEM((EARLY, 2, ROWS, CHANS), bf16),
+            pltpu.VMEM((EARLY, 2, ROWS, CHANS), bf16),
+            pltpu.VMEM((EARLY, 2, ROWS // 2, CHANS), bf16),
+            pltpu.VMEM((EARLY, 2, ROWS, CHANS), bf16),
+            pltpu.VMEM((EARLY, 8, CHANS), f32),
+            pltpu.VMEM((EARLY, 8, CHANS), f32),
             pltpu.SemaphoreType.DMA((CHUNKS,)),
             pltpu.SemaphoreType.DMA((6,)),
             pltpu.SemaphoreType.DMA((18,)),
@@ -323,8 +440,15 @@
             pltpu.SemaphoreType.DMA((PAIRS,)),
             pltpu.SemaphoreType.DMA((TM,)),
             pltpu.SemaphoreType.DMA((TM,)),
-            pltpu.SemaphoreType.DMA((CLIP,)),
-            pltpu.SemaphoreType.DMA((CLIP,)),
+            pltpu.SemaphoreType.DMA((SENDS,)),
+            pltpu.SemaphoreType.DMA((SENDS,)),
+            pltpu.SemaphoreType.DMA((EARLY,)),
+            pltpu.SemaphoreType.DMA((EARLY,)),
+            pltpu.SemaphoreType.DMA((EARLY,)),
+            pltpu.SemaphoreType.DMA((EARLY,)),
+            pltpu.SemaphoreType.DMA((EARLY,)),
+            pltpu.SemaphoreType.DMA((EARLY,)),
+            pltpu.SemaphoreType.DMA((EARLY,)),
         ],
         compiler_params=pltpu.CompilerParams(
             collective_id=0, has_side_effects=True, vmem_limit_bytes=40 << 20

time: 71.9 us -> 65.3 us (0.908)
  Pallas kernels: 69.8 us -> 63 us
    pallas_call x1, Pallas kernels: 69.8 us -> 63 us  [on_device(): pl.pallas_call(kernel, out_shape=jax.ShapeDtypeStruct((CLIP, 2, ROWS, CHA...]
where the time goes in v3:
time: 65.3 us; the launch traced here: 65 us
  Pallas kernels  63 us (96%)
  local copies, waits for them, and re-layouts  2.02 us (3%)
    pallas_call x1, Pallas kernels, on_device(): pl.pallas_call(kernel, out_shape=jax.ShapeDtypeStruct((CLIP, 2, ROWS, CHA...  63 us
    unnamed x1, local copies, waits for them, and re-layouts  2.02 us

profile of v3, /device:TPU:1, one launch (start us, length us, event | category | flops | bytes accessed | tf_op | source)
XLA Modules:
  0.0 65.0 jit_solution(3227380383604803028)
XLA Ops:
  0.0 63.0 %encode_and_send.1 = bf16[32,2,256,128]{3,2,1,0:T(8,128)(2,1)S(1)} custom-call(bf16[32,256,128]{2,1,0:T(8,128)(2,1)} %bitcast.8, s32[1,32]{1,0:T(1,128)} %bitcast.10, s32[1,32]{1,0:T(1,128)} %bitcast.9, s32[32]{0:T(128)} %frames_hbm.1, f32[1,128]{1,0:T(1,128)} %bitcast.11, f32[1,128]{1,0:T(1,128)} %bitcast.12, bf16[3,3,3,128,128]{4,3,2,1,0:T(8,128)(2,1)} %w_hbm.1, ...), custom_call_target="tpu_custom_call" | custom-call | tf_op jit(solution)/shard_map/encode_and_send/pallas_call | solution.py:405
  63.0 2.0 %copy.9 = bf16[64,4,8,8,128]{4,3,2,1,0:T(8,128)(2,1)} copy(bf16[64,4,8,8,128]{4,3,2,1,0:T(8,128)(2,1)S(1)} %bitcast.7) | data formatting | bytes 8388608

commit v4 on v3

--- a/solution.py
+++ b/solution.py
@@ -11,8 +11,29 @@
 ROWS = 4 * CELLS
 PAIRS = TILES // 2
 CHUNKS = 4
-EARLY = 4
+EARLY = 6
 SENDS = CLIP - 1 - EARLY
+
+
+SETS = [
+    [(2, 2)],
+    [(1, 1), (3, 3)],
+    [(1, 3), (3, 1)],
+    [(2, 0), (0, 2)],
+    [(1, 2), (3, 0)],
+    [(3, 2), (1, 0)],
+    [(2, 1), (0, 3)],
+    [(2, 3), (0, 1)],
+]
+ORDER = [(dx, dz, dc) for s in SETS for dc in range(2) for dx, dz in s] + [(0, 0, 1)]
+assert sorted(ORDER) == [(x, z, c) for x in range(4) for z in range(4) for c in range(2)][1:]
+
+
+def packed(values):
+    return [sum(v << 2 * i for i, v in enumerate(values[h : h + 15])) for h in (0, 15, 30)]
+
+
+WORDS = [packed([o[i] for o in ORDER]) for i in range(3)]
 
 
 def here():
@@ -20,29 +41,31 @@
     return lax.div(me, 8), lax.rem(lax.div(me, 2), 4), lax.rem(me, 2)
 
 
+def offset(k):
+    part, by = lax.div(k, 15), 2 * lax.rem(k, 15)
+    words = [jnp.where(part == 0, w[0], jnp.where(part == 1, w[1], w[2])) for w in WORDS]
+    return [lax.rem(lax.shift_right_logical(w, by), 4) for w in words]
+
+
 def target(k):
     x, z, core = here()
-    dc, a = lax.div(k, 16), lax.rem(k, 16)
-    dx = lax.rem(a, 4)
-    dz = a + lax.div(a, 4)
+    dx, dz, dc = offset(jnp.int32(k))
     return (lax.rem(x + dx, 4) * 4 + lax.rem(z + dz, 4)) * 2 + lax.rem(core + dc, 2)
 
 
 def origin(k):
     x, z, core = here()
-    dc, a = lax.div(k, 16), lax.rem(k, 16)
-    dx = lax.rem(a, 4)
-    dz = lax.rem(a + lax.div(a, 4), 4)
+    dx, dz, dc = offset(jnp.int32(k))
     return (lax.rem(x + 4 - dx, 4) * 4 + lax.rem(z + 4 - dz, 4)) * 2 + lax.rem(core + 2 - dc, 2)
 
 
 def place_of(group):
     x, z, core = here()
-    dc = (group % 2 - core + 2) % 2
-    dx = (group // 8 - x + 4) % 4
-    dz = ((group // 2) % 4 - z + 4) % 4
-    k = dc * 16 + dx + 4 * ((dz - dx + 4) % 4)
-    return (k + 31 - EARLY) % 32
+    step = jnp.full(group.shape, SENDS, jnp.int32)
+    for k, (dx, dz, dc) in enumerate(ORDER):
+        there = (lax.rem(x + dx, 4) * 4 + lax.rem(z + dz, 4)) * 2 + lax.rem(core + dc, 2)
+        step = jnp.where(group == there, k - EARLY if k >= EARLY else SENDS + 1 + k, step)
+    return step
 
 
 def group_sum(v):
@@ -86,10 +109,10 @@
         x_copies[q].start()
 
     barrier = pltpu.get_barrier_semaphore()
-    for k in range(1, CLIP):
-        pl.semaphore_signal(
-            barrier, inc=1, device_id={"clip": target(jnp.int32(k))}, device_id_type=MESH
-        )
+    x, z, core = here()
+    for dx, dz, dc in ORDER:
+        there = (lax.rem(x + dx, 4) * 4 + lax.rem(z + dz, 4)) * 2 + lax.rem(core + dc, 2)
+        pl.semaphore_signal(barrier, inc=1, device_id={"clip": there}, device_id_type=MESH)
     for d in range(1, TM):
         there = lax.rem(pos + d, TM)
         pl.semaphore_signal(barrier, inc=1, device_id={"tm": there}, device_id_type=MESH)
@@ -141,7 +164,7 @@
             dst_ref=raw_in.at[j],
             send_sem=raw_ssem.at[j],
             recv_sem=raw_rsem.at[j],
-            device_id={"clip": target(j + 1)},
+            device_id={"clip": target(j)},
             device_id_type=MESH,
         )
 
@@ -240,7 +263,7 @@
             dst_ref=out_ref.at[me],
             send_sem=out_ssem.at[i],
             recv_sem=out_rsem.at[i],
-            device_id={"clip": target(i + 1 + EARLY)},
+            device_id={"clip": target(i + EARLY)},
             device_id_type=MESH,
         )
 
@@ -309,7 +332,7 @@
             dst_ref=notes_in.at[j],
             send_sem=notes_ssem.at[j],
             recv_sem=notes_rsem.at[j],
-            device_id={"clip": target(j + 1)},
+            device_id={"clip": target(j)},
             device_id_type=MESH,
         )
 
@@ -355,7 +378,7 @@
     own.start()
 
     def late_out(j):
-        return pltpu.make_async_copy(late_done.at[j], out_ref.at[origin(j + 1)], late_sem.at[j])
+        return pltpu.make_async_copy(late_done.at[j], out_ref.at[origin(j)], late_sem.at[j])
 
     @pl.loop(0, EARLY)
     def _(j):

time: 65.3 us -> 61.3 us (0.939)
  Pallas kernels: 63 us -> 59.2 us
    pallas_call x1, Pallas kernels: 63 us -> 59.2 us  [on_device(): pl.pallas_call(kernel, out_shape=jax.ShapeDtypeStruct((CLIP, 2, ROWS, CHA...]
where the time goes in v4:
time: 61.3 us; the launch traced here: 61.2 us
  Pallas kernels  59.2 us (97%)
  local copies, waits for them, and re-layouts  2.02 us (3%)
    pallas_call x1, Pallas kernels, on_device(): pl.pallas_call(kernel, out_shape=jax.ShapeDtypeStruct((CLIP, 2, ROWS, CHA...  59.2 us
    unnamed x1, local copies, waits for them, and re-layouts  2.02 us

profile of v4, /device:TPU:1, one launch (start us, length us, event | category | flops | bytes accessed | tf_op | source)
XLA Modules:
  0.0 61.2 jit_solution(15320490584819828860)
XLA Ops:
  0.0 59.2 %encode_and_send.1 = bf16[32,2,256,128]{3,2,1,0:T(8,128)(2,1)S(1)} custom-call(bf16[32,256,128]{2,1,0:T(8,128)(2,1)} %bitcast.8, s32[1,32]{1,0:T(1,128)} %bitcast.10, s32[1,32]{1,0:T(1,128)} %bitcast.9, s32[32]{0:T(128)} %frames_hbm.1, f32[1,128]{1,0:T(1,128)} %bitcast.11, f32[1,128]{1,0:T(1,128)} %bitcast.12, bf16[3,3,3,128,128]{4,3,2,1,0:T(8,128)(2,1)} %w_hbm.1, ...), custom_call_target="tpu_custom_call" | custom-call | tf_op jit(solution)/shard_map/encode_and_send/pallas_call | solution.py:428
  59.2 2.0 %copy.9 = bf16[64,4,8,8,128]{4,3,2,1,0:T(8,128)(2,1)} copy(bf16[64,4,8,8,128]{4,3,2,1,0:T(8,128)(2,1)S(1)} %bitcast.7) | data formatting | bytes 8388608

commit v5 on v4

--- a/solution.py
+++ b/solution.py
@@ -11,19 +11,19 @@
 ROWS = 4 * CELLS
 PAIRS = TILES // 2
 CHUNKS = 4
-EARLY = 6
+EARLY = 8
 SENDS = CLIP - 1 - EARLY
 
 
 SETS = [
+    [(2, 3), (0, 1)],
     [(2, 2)],
-    [(1, 1), (3, 3)],
-    [(1, 3), (3, 1)],
+    [(2, 1), (0, 3)],
     [(2, 0), (0, 2)],
     [(1, 2), (3, 0)],
+    [(1, 3), (3, 1)],
     [(3, 2), (1, 0)],
-    [(2, 1), (0, 3)],
-    [(2, 3), (0, 1)],
+    [(1, 1), (3, 3)],
 ]
 ORDER = [(dx, dz, dc) for s in SETS for dc in range(2) for dx, dz in s] + [(0, 0, 1)]
 assert sorted(ORDER) == [(x, z, c) for x in range(4) for z in range(4) for c in range(2)][1:]

time: 61.3 us -> 60.7 us (level)
  no operation moved by 1% of the time
where the time goes in v5:
time: 60.7 us; the launch traced here: 60.6 us
  Pallas kernels  58.6 us (97%)
  local copies, waits for them, and re-layouts  2.02 us (3%)
    pallas_call x1, Pallas kernels, on_device(): pl.pallas_call(kernel, out_shape=jax.ShapeDtypeStruct((CLIP, 2, ROWS, CHA...  58.6 us
    unnamed x1, local copies, waits for them, and re-layouts  2.02 us

profile of v5, /device:TPU:1, one launch (start us, length us, event | category | flops | bytes accessed | tf_op | source)
XLA Modules:
  0.0 60.6 jit_solution(16276181525487600387)
XLA Ops:
  0.0 58.6 %encode_and_send.1 = bf16[32,2,256,128]{3,2,1,0:T(8,128)(2,1)S(1)} custom-call(bf16[32,256,128]{2,1,0:T(8,128)(2,1)} %bitcast.8, s32[1,32]{1,0:T(1,128)} %bitcast.10, s32[1,32]{1,0:T(1,128)} %bitcast.9, s32[32]{0:T(128)} %frames_hbm.1, f32[1,128]{1,0:T(1,128)} %bitcast.11, f32[1,128]{1,0:T(1,128)} %bitcast.12, bf16[3,3,3,128,128]{4,3,2,1,0:T(8,128)(2,1)} %w_hbm.1, ...), custom_call_target="tpu_custom_call" | custom-call | tf_op jit(solution)/shard_map/encode_and_send/pallas_call | solution.py:428
  58.6 2.0 %copy.9 = bf16[64,4,8,8,128]{4,3,2,1,0:T(8,128)(2,1)} copy(bf16[64,4,8,8,128]{4,3,2,1,0:T(8,128)(2,1)S(1)} %bitcast.7) | data formatting | bytes 8388608

commit v6 on v5

--- a/solution.py
+++ b/solution.py
@@ -226,7 +226,11 @@
     def _(m):
         for i in range(2):
             halo_out[m, i] = x_s[table[0, 2 * m + i], ROWS // 2 : ROWS, :]
-        halo_copy(m).start()
+
+        @pl.when(pos < TM - 1)
+        def _():
+            halo_copy(m).start()
+
 
     for copy in small_copies[1:]:
         copy.wait()
@@ -348,7 +352,11 @@
 
     @pl.loop(0, PAIRS)
     def _(m):
-        halo_copy(m).wait_recv()
+
+        @pl.when(pos > 0)
+        def _():
+            halo_copy(m).wait_recv()
+
         tiles = [table[0, 2 * m + i] for i in range(2)]
         results = unit(
             [
@@ -366,7 +374,11 @@
         @pl.when(m >= PAIRS - EARLY)
         def _():
             raw_copy(m - (PAIRS - EARLY)).wait_recv()
-            late_copy(m - (PAIRS - EARLY)).start()
+
+            @pl.when(pos < TM - 1)
+            def _():
+                late_copy(m - (PAIRS - EARLY)).start()
+
 
     @pl.loop(PAIRS, SENDS)
     def _(i):
@@ -382,7 +394,11 @@
 
     @pl.loop(0, EARLY)
     def _(j):
-        late_copy(j).wait_recv()
+
+        @pl.when(pos > 0)
+        def _():
+            late_copy(j).wait_recv()
+
         notes_copy(j).wait_recv()
         results = unit(
             [
@@ -401,12 +417,20 @@
 
     @pl.loop(0, PAIRS)
     def _(m):
-        halo_copy(m).wait_send()
+
+        @pl.when(pos < TM - 1)
+        def _():
+            halo_copy(m).wait_send()
+
 
     @pl.loop(0, EARLY)
     def _(j):
         raw_copy(j).wait_send()
-        late_copy(j).wait_send()
+
+        @pl.when(pos < TM - 1)
+        def _():
+            late_copy(j).wait_send()
+
         notes_copy(j).wait_send()
         late_out(j).wait()
 

time: 60.7 us -> 60.7 us (level)
  no operation moved by 1% of the time
where the time goes in v6:
time: 60.7 us; the launch traced here: 60.6 us
  Pallas kernels  58.6 us (97%)
  local copies, waits for them, and re-layouts  2.02 us (3%)
    pallas_call x1, Pallas kernels, on_device(): pl.pallas_call(kernel, out_shape=jax.ShapeDtypeStruct((CLIP, 2, ROWS, CHA...  58.6 us
    unnamed x1, local copies, waits for them, and re-layouts  2.02 us

profile of v6, /device:TPU:1, one launch (start us, length us, event | category | flops | bytes accessed | tf_op | source)
XLA Modules:
  0.0 60.6 jit_solution(10864021559930747950)
XLA Ops:
  0.0 58.6 %encode_and_send.1 = bf16[32,2,256,128]{3,2,1,0:T(8,128)(2,1)S(1)} custom-call(bf16[32,256,128]{2,1,0:T(8,128)(2,1)} %bitcast.8, s32[1,32]{1,0:T(1,128)} %bitcast.10, s32[1,32]{1,0:T(1,128)} %bitcast.9, s32[32]{0:T(128)} %frames_hbm.1, f32[1,128]{1,0:T(1,128)} %bitcast.11, f32[1,128]{1,0:T(1,128)} %bitcast.12, bf16[3,3,3,128,128]{4,3,2,1,0:T(8,128)(2,1)} %w_hbm.1, ...), custom_call_target="tpu_custom_call" | custom-call | tf_op jit(solution)/shard_map/encode_and_send/pallas_call | solution.py:452
  58.6 2.0 %copy.9 = bf16[64,4,8,8,128]{4,3,2,1,0:T(8,128)(2,1)} copy(bf16[64,4,8,8,128]{4,3,2,1,0:T(8,128)(2,1)S(1)} %bitcast.7) | data formatting | bytes 8388608

commit v7 on v6

--- a/solution.py
+++ b/solution.py
@@ -177,15 +177,12 @@
     for copy in x_copies:
         copy.wait()
 
+    pl.semaphore_wait(barrier, CLIP - 1 + TM - 1)
+
     @pl.loop(0, EARLY)
     def _(j):
         for i, (t, _) in enumerate(early_slots(j)):
             raw_out[j, i] = x_s[t]
-
-    pl.semaphore_wait(barrier, CLIP - 1 + TM - 1)
-
-    @pl.loop(0, EARLY)
-    def _(j):
         raw_copy(j).start()
 
     def stat_copy(d, there):

time: 60.7 us -> 60.7 us (level)
  no operation moved by 1% of the time
where the time goes in v7:
time: 60.7 us; the launch traced here: 60.6 us
  Pallas kernels  58.6 us (97%)
  local copies, waits for them, and re-layouts  2.02 us (3%)
    pallas_call x1, Pallas kernels, on_device(): pl.pallas_call(kernel, out_shape=jax.ShapeDtypeStruct((CLIP, 2, ROWS, CHA...  58.6 us
    unnamed x1, local copies, waits for them, and re-layouts  2.02 us

profile of v7, /device:TPU:1, one launch (start us, length us, event | category | flops | bytes accessed | tf_op | source)
XLA Modules:
  0.0 60.6 jit_solution(9813500323193559681)
XLA Ops:
  0.0 58.6 %encode_and_send.1 = bf16[32,2,256,128]{3,2,1,0:T(8,128)(2,1)S(1)} custom-call(bf16[32,256,128]{2,1,0:T(8,128)(2,1)} %bitcast.8, s32[1,32]{1,0:T(1,128)} %bitcast.10, s32[1,32]{1,0:T(1,128)} %bitcast.9, s32[32]{0:T(128)} %frames_hbm.1, f32[1,128]{1,0:T(1,128)} %bitcast.11, f32[1,128]{1,0:T(1,128)} %bitcast.12, bf16[3,3,3,128,128]{4,3,2,1,0:T(8,128)(2,1)} %w_hbm.1, ...), custom_call_target="tpu_custom_call" | custom-call | tf_op jit(solution)/shard_map/encode_and_send/pallas_call | solution.py:449
  58.6 2.0 %copy.9 = bf16[64,4,8,8,128]{4,3,2,1,0:T(8,128)(2,1)} copy(bf16[64,4,8,8,128]{4,3,2,1,0:T(8,128)(2,1)S(1)} %bitcast.7) | data formatting | bytes 8388608
